TPU v7x, 512 devices: a whole 4x4x16 slice. The times are simulated.
512 devices in a mesh: video: 16 (over x_hi, y, core), seq: 32 (over z, x_lo).
Axes of the slice: x: 4 (x_hi: 2, x_lo: 2; x = x_hi * 2 + x_lo), y: 4, z: 16, core: 2. Of those that a mesh axis runs over, the one named last changes fastest.
Arguments:
- queries: bfloat16 [262144, 1152], P(('video', 'seq')), parts along dimension 0, may hold values from -6 to 6
- key_vectors: bfloat16 [262144, 1152], P(('video', 'seq')), parts along dimension 0, may hold values from -6 to 6
- values_in: bfloat16 [262144, 1152], P(('video', 'seq')), parts along dimension 0, may hold values from -6 to 6
- norm_gain: float32 [1152], replicated, may hold values from 0.1 to 1.9
- state_weight: bfloat16 [1152, 256], replicated, may hold values from -0.1875 to 0.1875
- step_weight: bfloat16 [1152, 32], replicated, may hold values from -0.1875 to 0.1875
- step_bias: float32 [32], replicated, may hold values from -1 to 1
- decay_rate: float32 [32], replicated, may hold values from 0.005 to 0.2
Outputs:
- block_output: bfloat16 [262144, 1152], P(('video', 'seq')), parts along dimension 0
There are 16 independent parts, one for each index of `video`. A program takes and returns all parts, laid end to end along the dimension named above; an argument that names none is the same for every part. Nothing has to cross between parts.
All inputs are finite; a program needn't handle non-finite values.
Results may differ from a plain program's by a relative error of at most 0.011.
Values may be sent and summed in bfloat16 or wider, within the bound.
A program may use at most 64 MiB of HBM per device.

v0:
```python
import jax
import jax.numpy as jnp
from jax import lax
from jax.sharding import PartitionSpec as P

HEADS = 16
HEAD = 72


EPSILON = 1e-06


def attend_frame(query_rows, key_rows, value_rows):
    tokens = query_rows.shape[0]
    per_turn = 4
    turns = HEADS // per_turn
    query_groups = jnp.transpose(query_rows.reshape(tokens, turns, per_turn, HEAD), (1, 0, 2, 3))
    key_groups = jnp.transpose(key_rows.reshape(tokens, turns, per_turn, HEAD), (1, 0, 2, 3))
    value_groups = jnp.transpose(value_rows.reshape(tokens, turns, per_turn, HEAD), (1, 0, 2, 3))

    def one_group(group_inputs):
        query_heads, key_heads, value_heads = group_inputs
        scores = jnp.einsum(
            "qhe,khe->hqk", query_heads, key_heads, preferred_element_type=jnp.float32
        ) * HEAD ** (-0.5)
        row_max = jnp.max(scores, axis=-1, keepdims=True)
        exponent = jnp.exp(scores - row_max)
        probabilities = (exponent / jnp.sum(exponent, axis=-1, keepdims=True)).astype(jnp.bfloat16)
        attended = jnp.einsum(
            "hqk,khe->qhe", probabilities, value_heads, preferred_element_type=jnp.float32
        )
        return attended.astype(jnp.bfloat16)

    outputs = lax.map(one_group, (query_groups, key_groups, value_groups))
    return jnp.transpose(outputs, (1, 0, 2, 3)).reshape(tokens, HEADS * HEAD)


def normalize(attended, norm_gain):
    widened = attended.astype(jnp.float32)
    mean_square = jnp.mean(widened * widened, axis=-1, keepdims=True)
    return (widened * lax.rsqrt(mean_square + EPSILON) * norm_gain).astype(jnp.bfloat16)


def project(normed_rows, state_weight, step_weight):
    state_total = jnp.dot(normed_rows, state_weight, preferred_element_type=jnp.float32)
    step_total = jnp.dot(normed_rows, step_weight, preferred_element_type=jnp.float32)
    return (state_total.astype(jnp.bfloat16), step_total.astype(jnp.bfloat16))


def temporal_mix(normed, state_proj, step_proj, step_bias, decay_rate):
    frames, patches, channels = normed.shape
    head_count = step_proj.shape[2] // 2
    state_size = state_proj.shape[2] // 4
    step_size = jax.nn.softplus(step_proj.astype(jnp.float32) + step_bias)
    forward_step = step_size[..., :head_count]
    backward_step = step_size[..., head_count:]
    forward_total = jnp.cumsum(forward_step, axis=0)
    backward_total = jnp.flip(jnp.cumsum(jnp.flip(backward_step, 0), axis=0), 0)
    input_fwd = state_proj[..., :state_size]
    output_fwd = state_proj[..., state_size : 2 * state_size]
    input_bwd = state_proj[..., 2 * state_size : 3 * state_size]
    output_bwd = state_proj[..., 3 * state_size :]
    gram_forward = jnp.einsum(
        "tpn,spn->pts", output_fwd, input_fwd, preferred_element_type=jnp.float32
    ) * state_size ** (-0.5)
    gram_backward = jnp.einsum(
        "tpn,spn->pts", output_bwd, input_bwd, preferred_element_type=jnp.float32
    ) * state_size ** (-0.5)
    positions = jnp.arange(frames)
    causal_mask = positions[:, None] >= positions[None, :]
    anti_mask = positions[:, None] <= positions[None, :]
    forward_lead = jnp.transpose(forward_total, (1, 2, 0))
    backward_lead = jnp.transpose(backward_total, (1, 2, 0))
    forward_gap = forward_lead[..., :, None] - forward_lead[..., None, :]
    backward_gap = backward_lead[..., :, None] - backward_lead[..., None, :]
    forward_decay = jnp.where(
        causal_mask,
        jnp.exp(-decay_rate[:head_count, None, None] * jnp.where(causal_mask, forward_gap, 0.0)),
        0.0,
    )
    backward_decay = jnp.where(
        anti_mask,
        jnp.exp(-decay_rate[head_count:, None, None] * jnp.where(anti_mask, backward_gap, 0.0)),
        0.0,
    )
    forward_weight = (
        gram_forward[:, None]
        * forward_decay
        * jnp.transpose(forward_step, (1, 2, 0))[:, :, None, :]
    )
    backward_weight = (
        gram_backward[:, None]
        * backward_decay
        * jnp.transpose(backward_step, (1, 2, 0))[:, :, None, :]
    )
    scan_weights = (forward_weight + backward_weight).astype(jnp.bfloat16)
    normed_heads = normed.reshape(frames, patches, head_count, channels // head_count)
    carried = jnp.einsum(
        "phts,sphe->tphe", scan_weights, normed_heads, preferred_element_type=jnp.float32
    )
    return (normed.astype(jnp.float32) + carried.reshape(frames, patches, channels)).astype(
        jnp.bfloat16
    )


def send_back(mixed):
    return lax.all_to_all(mixed, "seq", split_axis=0, concat_axis=0, tiled=True)


def shards(
    queries, key_vectors, values_in, norm_gain, state_weight, step_weight, step_bias, decay_rate
):
    attended = attend_frame(queries, key_vectors, values_in)
    tokens, channels = attended.shape
    groups = lax.axis_size("seq")
    per_group = tokens // groups
    normed = normalize(attended, norm_gain)
    state_proj, step_proj = project(normed, state_weight, step_weight)
    result = send_back(
        temporal_mix(
            lax.all_to_all(
                normed.reshape(groups, per_group, channels),
                "seq",
                split_axis=0,
                concat_axis=0,
                tiled=True,
            ),
            lax.all_to_all(
                state_proj.reshape(groups, per_group, -1),
                "seq",
                split_axis=0,
                concat_axis=0,
                tiled=True,
            ),
            lax.all_to_all(
                step_proj.reshape(groups, per_group, -1),
                "seq",
                split_axis=0,
                concat_axis=0,
                tiled=True,
            ),
            step_bias,
            decay_rate,
        )
    )
    return result.reshape(tokens, channels)


def solution(mesh):
    in_specs = (
        P(("video", "seq"), None),
        P(("video", "seq"), None),
        P(("video", "seq"), None),
        P(),
        P(),
        P(),
        P(),
        P(),
    )
    out_specs = P(("video", "seq"), None)
    return jax.shard_map(shards, mesh=mesh, in_specs=in_specs, out_specs=out_specs, check_vma=False)
```

profile of v0, /device:TPU:24, one launch (start us, length us, event | category | flops | bytes accessed | tf_op | source)
XLA Modules:
  0.0 242.6 jit_solution(13022634934928212138)
XLA Ops:
  0.0 2.5 %copy.24 = bf16[512,1152]{0,1:T(8,128)(2,1)} copy(bf16[512,1152]{1,0:T(8,128)(2,1)} %param.11) | data formatting | bytes 2359296 | tf_op args[1]
  5.5 28.8 %while.10 = (s32[]{:T(128)}, bf16[4,512,4,72]{1,3,2,0:T(8,128)(2,1)S(1)}, bf16[4,512,4,72]{1,3,2,0:T(8,128)(2,1)}, bf16[4,512,4,72]{1,3,2,0:T(8,128)(2,1)S(1)}, bf16[4,512,4,72]{1,3,2,0:T(8,128)(2,1)}, /*index=5*/s32[]{:T(128)}) while((s32[]{:T(128)}, bf16[4,512,4,72]{1,3,2,0:T(8,128)(2,1)S(1)}, bf16[4,512,4,72]{1,3,2,0:T(8,128)(2,1)}, ...), condition=%wide.region_3.4_spmd, body=%wide.region_0.3_spmd.sunk | while | flops 307380736 | bytes 9586757 | solution.py:34
  5.5 4.4 %fusion.84 = (f32[4,512]{1,0:T(4,128)S(1)}, f32[4,512,512]{1,2,0:T(8,128)}) fusion(bf16[4,512,4,72]{1,3,2,0:T(8,128)(2,1)} %get-tuple-element.107, s32[]{:T(128)} %get-tuple-element.97, bf16[4,512,4,72]{1,3,2,0:T(8,128)(2,1)S(1)} %get-tuple-element.106), kind=kOutput, calls=%fused_computation.69.clone.1 | convolution fusion | flops 154141184 | bytes 4793344 | tf_op jit(solution)/shard_map/while/body/eval_jaxpr/sub | solution.py:27
  9.9 2.8 %fusion.85 = bf16[4,512,4,72]{1,3,2,0:T(8,128)(2,1)S(1)} fusion(bf16[4,512,4,72]{1,3,2,0:T(8,128)(2,1)S(1)} %get-tuple-element.98, s32[]{:T(128)} %get-tuple-element.97, f32[4,512,512]{1,2,0:T(8,128)} %get-tuple-element.89, f32[4,512]{1,0:T(4,128)S(1)} %get-tuple-element.90, bf16[4,512,4,72]{1,3,2,0:T(8,128)(2,1)} %get-tuple-element.105), kind=kOutput, calls=%fused_computation.9.clone.1 | convolution fusion | flops 153239552 | bytes 4793344 | tf_op jit(solution)/shard_map/while/body/eval_jaxpr/hqk,khe->qhe/dot_general | solution.py:29
  12.7 4.4 %fusion.84 = (f32[4,512]{1,0:T(4,128)S(1)}, f32[4,512,512]{1,2,0:T(8,128)}) fusion(bf16[4,512,4,72]{1,3,2,0:T(8,128)(2,1)} %get-tuple-element.107, s32[]{:T(128)} %get-tuple-element.97, bf16[4,512,4,72]{1,3,2,0:T(8,128)(2,1)S(1)} %get-tuple-element.106), kind=kOutput, calls=%fused_computation.69.clone.1 | convolution fusion | flops 154141184 | bytes 4793344 | tf_op jit(solution)/shard_map/while/body/eval_jaxpr/sub | solution.py:27
  17.2 2.8 %fusion.85 = bf16[4,512,4,72]{1,3,2,0:T(8,128)(2,1)S(1)} fusion(bf16[4,512,4,72]{1,3,2,0:T(8,128)(2,1)S(1)} %get-tuple-element.98, s32[]{:T(128)} %get-tuple-element.97, f32[4,512,512]{1,2,0:T(8,128)} %get-tuple-element.89, f32[4,512]{1,0:T(4,128)S(1)} %get-tuple-element.90, bf16[4,512,4,72]{1,3,2,0:T(8,128)(2,1)} %get-tuple-element.105), kind=kOutput, calls=%fused_computation.9.clone.1 | convolution fusion | flops 153239552 | bytes 4793344 | tf_op jit(solution)/shard_map/while/body/eval_jaxpr/hqk,khe->qhe/dot_general | solution.py:29
  19.9 4.4 %fusion.84 = (f32[4,512]{1,0:T(4,128)S(1)}, f32[4,512,512]{1,2,0:T(8,128)}) fusion(bf16[4,512,4,72]{1,3,2,0:T(8,128)(2,1)} %get-tuple-element.107, s32[]{:T(128)} %get-tuple-element.97, bf16[4,512,4,72]{1,3,2,0:T(8,128)(2,1)S(1)} %get-tuple-element.106), kind=kOutput, calls=%fused_computation.69.clone.1 | convolution fusion | flops 154141184 | bytes 4793344 | tf_op jit(solution)/shard_map/while/body/eval_jaxpr/sub | solution.py:27
  24.4 2.8 %fusion.85 = bf16[4,512,4,72]{1,3,2,0:T(8,128)(2,1)S(1)} fusion(bf16[4,512,4,72]{1,3,2,0:T(8,128)(2,1)S(1)} %get-tuple-element.98, s32[]{:T(128)} %get-tuple-element.97, f32[4,512,512]{1,2,0:T(8,128)} %get-tuple-element.89, f32[4,512]{1,0:T(4,128)S(1)} %get-tuple-element.90, bf16[4,512,4,72]{1,3,2,0:T(8,128)(2,1)} %get-tuple-element.105), kind=kOutput, calls=%fused_computation.9.clone.1 | convolution fusion | flops 153239552 | bytes 4793344 | tf_op jit(solution)/shard_map/while/body/eval_jaxpr/hqk,khe->qhe/dot_general | solution.py:29
  27.2 4.4 %fusion.84 = (f32[4,512]{1,0:T(4,128)S(1)}, f32[4,512,512]{1,2,0:T(8,128)}) fusion(bf16[4,512,4,72]{1,3,2,0:T(8,128)(2,1)} %get-tuple-element.107, s32[]{:T(128)} %get-tuple-element.97, bf16[4,512,4,72]{1,3,2,0:T(8,128)(2,1)S(1)} %get-tuple-element.106), kind=kOutput, calls=%fused_computation.69.clone.1 | convolution fusion | flops 154141184 | bytes 4793344 | tf_op jit(solution)/shard_map/while/body/eval_jaxpr/sub | solution.py:27
  31.6 2.8 %fusion.85 = bf16[4,512,4,72]{1,3,2,0:T(8,128)(2,1)S(1)} fusion(bf16[4,512,4,72]{1,3,2,0:T(8,128)(2,1)S(1)} %get-tuple-element.98, s32[]{:T(128)} %get-tuple-element.97, f32[4,512,512]{1,2,0:T(8,128)} %get-tuple-element.89, f32[4,512]{1,0:T(4,128)S(1)} %get-tuple-element.90, bf16[4,512,4,72]{1,3,2,0:T(8,128)(2,1)} %get-tuple-element.105), kind=kOutput, calls=%fused_computation.9.clone.1 | convolution fusion | flops 153239552 | bytes 4793344 | tf_op jit(solution)/shard_map/while/body/eval_jaxpr/hqk,khe->qhe/dot_general | solution.py:29
  36.5 16.4 %all-to-all-start.2 = ((bf16[32,2,256]{2,1,0:T(2,128)(2,1)}), bf16[32,2,256]{2,1,0:T(2,128)(2,1)S(1)}, u32[]{:S(2)}, u32[]{:S(2)}) async-start(bf16[32,2,256]{2,1,0:T(2,128)(2,1)} %reshape.83), calls=%async_computation.2 | async-start | bytes 65536 | tf_op jit(solution)/shard_map/all_to_all | solution.py:135
  54.1 12.1 %all-to-all-done.2 = bf16[32,2,256]{2,1,0:T(2,128)(2,1)S(1)} async-done(((bf16[32,2,256]{2,1,0:T(2,128)(2,1)}), bf16[32,2,256]{2,1,0:T(2,128)(2,1)S(1)}, u32[]{:S(2)}, u32[]{:S(2)}) %all-to-all-start.2) | async-done | bytes 32800 | tf_op jit(solution)/shard_map/all_to_all | solution.py:135
  66.3 3.9 %all-to-all-start.1 = ((bf16[32,16,256]{2,1,0:T(8,128)(2,1)}), bf16[32,16,256]{2,1,0:T(8,128)(2,1)S(1)}, u32[]{:S(2)}, u32[]{:S(2)}) async-start(bf16[32,16,256]{2,1,0:T(8,128)(2,1)} %bitcast.13), calls=%async_computation.1 | async-start | bytes 524288 | tf_op jit(solution)/shard_map/all_to_all | solution.py:128
  72.0 4.9 %copy.25 = f32[512,4,4,72]{3,2,1,0:T(4,128)} copy(f32[512,4,4,72]{0,3,2,1:T(8,128)} %convert_bitcast_fusion) | data formatting | bytes 4718592 | tf_op jit(solution)/shard_map/convert_element_type | solution.py:39
  76.9 6.0 %reshape.81 = f32[32,16,1152]{2,1,0:T(8,128)S(1)} reshape(f32[512,4,4,72]{3,2,1,0:T(4,128)} %copy.25) | data formatting | bytes 4718592 | tf_op jit(solution)/shard_map/convert_element_type | solution.py:39
  84.2 6.7 %all-to-all-done.1 = bf16[32,16,256]{2,1,0:T(8,128)(2,1)S(1)} async-done(((bf16[32,16,256]{2,1,0:T(8,128)(2,1)}), bf16[32,16,256]{2,1,0:T(8,128)(2,1)S(1)}, u32[]{:S(2)}, u32[]{:S(2)}) %all-to-all-start.1) | async-done | bytes 262176 | tf_op jit(solution)/shard_map/all_to_all | solution.py:128
  90.9 6.5 %all-to-all-start = ((bf16[32,16,1152]{2,1,0:T(8,128)(2,1)}), bf16[32,16,1152]{2,1,0:T(8,128)(2,1)S(1)}, u32[]{:S(2)}, u32[]{:S(2)}) async-start(bf16[32,16,1152]{2,1,0:T(8,128)(2,1)} %multiply_convert_fusion), calls=%async_computation | async-start | bytes 2359296 | tf_op jit(solution)/shard_map/all_to_all | solution.py:121
  101.2 54.2 %all-to-all-done = bf16[32,16,1152]{2,1,0:T(8,128)(2,1)S(1)} async-done(((bf16[32,16,1152]{2,1,0:T(8,128)(2,1)}), bf16[32,16,1152]{2,1,0:T(8,128)(2,1)S(1)}, u32[]{:S(2)}, u32[]{:S(2)}) %all-to-all-start) | async-done | bytes 1179680 | tf_op jit(solution)/shard_map/all_to_all | solution.py:121
  155.4 4.7 %reshape.76 = bf16[32,16,16,72]{3,2,1,0:T(8,128)(2,1)} reshape(bf16[32,16,1152]{2,1,0:T(8,128)(2,1)S(1)} %all-to-all-done) | data formatting | bytes 2359296 | tf_op jit(solution)/shard_map/reshape | solution.py:97
  160.1 5.0 %convolution_bitcast_fusion = f32[32,16,16,72]{3,0,2,1:T(8,128)S(1)} fusion(bf16[32,16,16,72]{3,2,1,0:T(8,128)(2,1)} %reshape.76, f32[16,16,32]{2,1,0:T(8,128)S(1)} %copy.32, f32[16,16,32]{2,1,0:T(8,128)S(1)} %copy.30, f32[16]{0:T(128)S(1)} %get-tuple-element.53, f32[16,32,32]{2,1,0:T(8,128)S(1)} %convolution_multiply_fusion, f32[16,16,32]{2,1,0:T(8,128)S(1)} %copy.29, ...), kind=kOutput, calls=%fused_computation.33 | convolution fusion | flops 41418752 | bytes 3803264 | tf_op jit(solution)/shard_map/phts,sphe->tphe/dot_general | solution.py:98
  165.1 4.4 %copy.34 = f32[32,16,16,72]{3,2,1,0:T(8,128)} copy(f32[32,16,16,72]{3,0,2,1:T(8,128)S(1)} %convolution_bitcast_fusion) | data formatting | bytes 4718592 | tf_op jit(solution)/shard_map/phts,sphe->tphe/transpose | solution.py:98
  169.5 5.2 %reshape.79 = f32[32,16,1152]{2,1,0:T(8,128)} reshape(f32[32,16,16,72]{3,2,1,0:T(8,128)} %copy.34) | data formatting | bytes 4718592 | tf_op jit(solution)/shard_map/reshape | solution.py:101
  174.7 1.9 add_convert_fusion.1
  176.6 65.0 %all_to_all.20 = bf16[32,16,1152]{2,1,0:T(8,128)(2,1)S(1)} all-to-all(bf16[32,16,1152]{2,1,0:T(8,128)(2,1)S(1)} %add_convert_fusion.1), channel_id=1, replica_groups=mesh['video'=16,'seq'=32] {'seq'}, dimensions={0} | all-to-all | bytes 2359296 | tf_op jit(solution)/shard_map/all_to_all | solution.py:107
  (42 shorter events, 14.1 us)
Async XLA Ops:
  0.0 52.9 %copy-start = (bf16[1152,256]{1,0:T(8,128)(2,1)S(1)}, bf16[1152,256]{1,0:T(8,128)(2,1)}, u32[]{:S(2)}) copy-start(bf16[1152,256]{1,0:T(8,128)(2,1)} %param.14) | copy-start | bytes 1769476
  0.0 2.5 %copy-start.1 = (bf16[512,1152]{1,0:T(8,128)(2,1)S(1)}, bf16[512,1152]{1,0:T(8,128)(2,1)}, u32[]{:S(2)}) copy-start(bf16[512,1152]{1,0:T(8,128)(2,1)} %param.12) | copy-start | bytes 3538948
  5.5 29.2 %copy-start.3 = (f32[1152]{0:T(1024)S(1)}, f32[1152]{0:T(1024)}, u32[]{:S(2)}) copy-start(f32[1152]{0:T(1024)} %param.13) | copy-start | bytes 13828
  34.4 0.9 copy-start.2
  36.5 29.8 %all-to-all-start.2 = ((bf16[32,2,256]{2,1,0:T(2,128)(2,1)}), bf16[32,2,256]{2,1,0:T(2,128)(2,1)S(1)}, u32[]{:S(2)}, u32[]{:S(2)}) async-start(bf16[32,2,256]{2,1,0:T(2,128)(2,1)} %reshape.83), calls=%async_computation.2 | async-start | bytes 65536 | tf_op jit(solution)/shard_map/all_to_all | solution.py:135
  66.3 24.7 %all-to-all-start.1 = ((bf16[32,16,256]{2,1,0:T(8,128)(2,1)}), bf16[32,16,256]{2,1,0:T(8,128)(2,1)S(1)}, u32[]{:S(2)}, u32[]{:S(2)}) async-start(bf16[32,16,256]{2,1,0:T(8,128)(2,1)} %bitcast.13), calls=%async_computation.1 | async-start | bytes 524288 | tf_op jit(solution)/shard_map/all_to_all | solution.py:128
  82.9 14.6 %copy-start.4 = (f32[32]{0:T(128)S(1)}, f32[32]{0:T(128)}, u32[]{:S(2)}) copy-start(f32[32]{0:T(128)} %param.17) | copy-start | bytes 388
  82.9 14.8 %copy-start.5 = (f32[32]{0:T(128)S(1)}, f32[32]{0:T(128)}, u32[]{:S(2)}) copy-start(f32[32]{0:T(128)} %param.16) | copy-start | bytes 388
  90.9 64.5 %all-to-all-start = ((bf16[32,16,1152]{2,1,0:T(8,128)(2,1)}), bf16[32,16,1152]{2,1,0:T(8,128)(2,1)S(1)}, u32[]{:S(2)}, u32[]{:S(2)}) async-start(bf16[32,16,1152]{2,1,0:T(8,128)(2,1)} %multiply_convert_fusion), calls=%async_computation | async-start | bytes 2359296 | tf_op jit(solution)/shard_map/all_to_all | solution.py:121
where the time goes:
time: 243 us
  waiting for transfers between devices  73.1 us (30%)
  blocking collectives  65 us (27%)
  matrix products  35.7 us (15%)
  local copies, waits for them, and re-layouts  34 us (14%)
  starting transfers between devices  26.8 us (11%)
  other arithmetic  7.74 us (3%)
    all_to_all x1, blocking collectives, send_back(): return lax.all_to_all(mixed, 'seq', split_axis=0, concat_axis=0, tiled=True)  65 us
    all_to_all x1, waiting for transfers between devices, shards(): lax.all_to_all(normed.reshape(groups, per_group, channels), 'seq', split_...  54.2 us
    sub x4, matrix products, one_group(): exponent = jnp.exp(scores - row_max)  17.6 us
    all_to_all x1, starting transfers between devices, shards(): lax.all_to_all(step_proj.reshape(groups, per_group, -1), 'seq', split_axi...  16.4 us
    all_to_all x1, waiting for transfers between devices, shards(): lax.all_to_all(step_proj.reshape(groups, per_group, -1), 'seq', split_axi...  12.1 us
    dot_general x4, matrix products, one_group(): jnp.einsum('hqk,khe->qhe', probabilities, value_heads, preferred_element_...  11.1 us
    convert_element_type x2, local copies, waits for them, and re-layouts, normalize(): widened = attended.astype(jnp.float32)  10.9 us
    unnamed x18, local copies, waits for them, and re-layouts  7.65 us
  transfers between devices with their start and end apart: 3, of which 3 were waited for; matrix products, arithmetic and copies ran while one was open for 8% of the time, Pallas kernels for 0%

commit v1 on v0

v1 whole, which is shorter than its diff:
```python
import functools

import jax
import jax.numpy as jnp
from jax import lax
from jax.experimental import pallas as pl
from jax.experimental.pallas import tpu as pltpu
from jax.sharding import PartitionSpec as P

HEADS = 16
HEAD = 72
STATE = 64
EPSILON = 1e-06
LOG2E = 1.4426950408889634
WINDOW = 256
MESH = pl.DeviceIdType.MESH
F32 = jnp.float32
BF16 = jnp.bfloat16


def window_of(head, channels):
    start = head * HEAD // 128 * 128
    if isinstance(head, int):
        start = min(start, channels - WINDOW)
    else:
        start = pl.multiple_of(jnp.minimum(start, channels - WINDOW), 128)
    return start, head * HEAD - start


def head_mask(rows, offset):
    lane = lax.broadcasted_iota(jnp.int32, (rows, WINDOW), 1)
    return (lane >= offset) & (lane < offset + HEAD)


def attend(q_ref, k_ref, v_ref, acc_ref, row, unroll):
    rows, channels = acc_ref.shape
    scale = HEAD ** (-0.5) * LOG2E

    def one_head(head, carry):
        start, offset = window_of(head, channels)
        lanes = pl.ds(start, WINDOW)
        mask = head_mask(rows, offset)
        query = jnp.where(mask, q_ref[pl.ds(row, rows), lanes], jnp.zeros((), BF16))
        scores = lax.dot_general(
            query, k_ref[:, lanes], (((1,), (1,)), ((), ())), preferred_element_type=F32
        )
        row_max = jnp.max(scores, axis=1, keepdims=True)
        exponent = jnp.exp2((scores - row_max) * scale)
        total = jnp.sum(exponent, axis=1, keepdims=True)
        mixed = jnp.dot(exponent.astype(BF16), v_ref[:, lanes], preferred_element_type=F32)
        acc_ref[:, lanes] = jnp.where(mask, mixed * (1.0 / total), acc_ref[:, lanes])
        return carry

    lax.fori_loop(0, HEADS, one_head, 0, unroll=unroll)


def normalize(attended, gain):
    widened = attended.astype(BF16).astype(F32)
    mean_square = jnp.mean(widened * widened, axis=1, keepdims=True)
    return (widened * lax.rsqrt(mean_square + EPSILON) * gain).astype(BF16)


def prepare_group(group, x_ref, xb_ref, sw_ref, tw_ref, bias_ref, decay_ref, gram_ref, lead_ref, lead_t_ref, step_t_ref):
    rows = gram_ref.shape[2]
    frames = rows // 4
    base = pl.multiple_of(group * rows, rows)
    for tile in range(x_ref.shape[0]):
        xb_ref[pl.ds(base, rows), pl.ds(tile * 128, 128)] = x_ref[tile, pl.ds(base, rows), :].astype(BF16)
    normed = xb_ref[pl.ds(base, rows), :]
    state = jnp.dot(normed, sw_ref[...], preferred_element_type=F32).astype(BF16)
    step = jnp.dot(normed, tw_ref[...], preferred_element_type=F32).astype(BF16).astype(F32)
    step = step + bias_ref[...]
    step = jnp.maximum(step, 0.0) + jnp.log1p(jnp.exp(-jnp.abs(step)))
    i = lax.broadcasted_iota(jnp.int32, (rows, rows), 0)
    j = lax.broadcasted_iota(jnp.int32, (rows, rows), 1)
    same = (i // frames) == (j // frames)
    causal, anti = same & (j <= i), same & (j >= i)
    nt = (((1,), (1,)), ((), ()))
    for direction, mask in ((0, causal), (1, anti)):
        lo = 2 * STATE * direction
        gram = lax.dot_general(
            state[:, lo + STATE : lo + 2 * STATE], state[:, lo : lo + STATE], nt, preferred_element_type=F32
        )
        gram_ref[group, direction] = jnp.where(mask, gram * STATE ** (-0.5), 0.0)
    hi = step.astype(BF16)
    low = (step - hi.astype(F32)).astype(BF16)
    sums = []
    for mask in (causal, anti):
        ones = jnp.where(mask, 1.0, 0.0).astype(BF16)
        sums.append(
            jnp.dot(ones, hi, preferred_element_type=F32) + jnp.dot(ones, low, preferred_element_type=F32)
        )
    column = lax.broadcasted_iota(jnp.int32, step.shape, 1)
    lead = jnp.where(column < HEADS, sums[0], sums[1]) * (decay_ref[...] * LOG2E)
    lead_ref[group] = lead
    lead_t_ref[group] = lead.T
    step_t_ref[group] = step.T


def mix_group(group, heads, xb_ref, y_ref, gram_ref, lead_ref, lead_t_ref, step_t_ref):
    rows = gram_ref.shape[2]
    channels = xb_ref.shape[1]
    base = pl.multiple_of(group * rows, rows)
    i = lax.broadcasted_iota(jnp.int32, (rows, rows), 0)
    j = lax.broadcasted_iota(jnp.int32, (rows, rows), 1)
    causal = j <= i
    for head in heads:
        back = HEADS + head
        gap = jnp.where(
            causal,
            lead_t_ref[group, head : head + 1, :] - lead_ref[group, :, head : head + 1],
            lead_t_ref[group, back : back + 1, :] - lead_ref[group, :, back : back + 1],
        )
        weight = jnp.exp2(jnp.minimum(gap, 0.0)) * (
            gram_ref[group, 0] * step_t_ref[group, head : head + 1, :]
            + gram_ref[group, 1] * step_t_ref[group, back : back + 1, :]
        )
        start, offset = window_of(head, channels)
        lanes = pl.ds(start, WINDOW)
        normed = xb_ref[pl.ds(base, rows), lanes]
        mixed = jnp.dot(weight.astype(BF16), normed, preferred_element_type=F32) + normed.astype(F32)
        mask = head_mask(rows, offset)
        for side in range(WINDOW // 128):
            own = slice(side * 128, side * 128 + 128)
            if offset < own.stop and offset + HEAD > own.start:
                place = (start // 128 + side, pl.ds(base, rows), slice(None))
                y_ref[place] = jnp.where(mask[:, own], mixed[:, own], y_ref[place])


def kernel(
    frames, chunks,
    q_hbm, k_hbm, v_hbm, gain_ref, sw_ref, tw_ref, bias_ref, decay_ref, o_ref,
    q_ref, k_ref, v_ref, acc_ref, out1_ref, in1_ref, x_ref, xb_ref, y_ref, gram_ref, lead_ref, lead_t_ref, step_t_ref, out2_ref,
    in_sem, send1, recv1, send2, recv2, own_sem,
):
    video, me = lax.axis_index("video"), lax.axis_index("seq")
    tokens, channels = out1_ref.shape
    per = tokens // frames
    half = frames // 2
    block = acc_ref.shape[0]

    loads = [
        pltpu.make_async_copy(source, target, in_sem.at[n])
        for n, (source, target) in enumerate(((q_hbm, q_ref), (k_hbm, k_ref), (v_hbm, v_ref)))
    ]
    for load in loads:
        load.start()
    barrier = pltpu.get_barrier_semaphore()

    def greet(k, carry):
        pl.semaphore_signal(
            barrier, inc=1, device_id=(video, lax.rem(me + k, frames)), device_id_type=MESH
        )
        return carry

    lax.fori_loop(1, frames, greet, 0)
    for load in loads:
        load.wait()

    def rows_of(index):
        return pl.ds(pl.multiple_of(index * per, per), per)

    def first_copy(target):
        return pltpu.make_async_remote_copy(
            src_ref=out1_ref.at[rows_of(target)],
            dst_ref=in1_ref.at[rows_of(me)],
            send_sem=send1.at[target],
            recv_sem=recv1.at[me],
            device_id=(video, target),
            device_id_type=MESH,
        )

    def first_arrival(source):
        return pltpu.make_async_remote_copy(
            src_ref=out1_ref.at[rows_of(source)],
            dst_ref=in1_ref.at[rows_of(source)],
            send_sem=send1.at[source],
            recv_sem=recv1.at[source],
            device_id=(video, source),
            device_id_type=MESH,
        )

    for turn in range(2):
        side = lax.rem(me // half + 1 + turn, 2)
        row = pl.multiple_of(side * block, block)
        attend(q_ref, k_ref, v_ref, acc_ref, row, 4)
        out1_ref[pl.ds(row, block), :] = normalize(acc_ref[...], gain_ref[...])
        if turn == 0:
            pl.semaphore_wait(barrier, frames - 1)

        def send(k, carry, side=side):
            first_copy(side * half + lax.rem(me + k, half)).start()
            return carry

        lax.fori_loop(turn, half, send, 0)

    def place_rows(rows, source):
        rows = rows.astype(F32)
        for tile in range(channels // 128):
            x_ref[tile, pl.ds(source, per, stride=frames), :] = rows[:, tile * 128 : tile * 128 + 128]

    def spread(source):
        place_rows(in1_ref[rows_of(source), :], source)

    place_rows(out1_ref[rows_of(me), :], me)
    for turn in range(2):
        side = lax.rem(me // half + 1 + turn, 2)

        def arrive(k, carry, side=side):
            source = side * half + lax.rem(me + half - k, half)
            first_arrival(source).wait_recv()
            spread(source)
            return carry

        lax.fori_loop(turn, half, arrive, 0)

    groups = gram_ref.shape[0]

    def prepare(group, carry):
        prepare_group(
            group, x_ref, xb_ref, sw_ref, tw_ref, bias_ref, decay_ref, gram_ref, lead_ref, lead_t_ref, step_t_ref
        )
        return carry

    lax.fori_loop(0, groups, prepare, 0)

    def second_copy(n, target):
        lanes = pl.ds(chunks[n][0], chunks[n][1])
        return pltpu.make_async_remote_copy(
            src_ref=out2_ref.at[rows_of(target), lanes],
            dst_ref=o_ref.at[rows_of(me), lanes],
            send_sem=send2.at[n, target],
            recv_sem=recv2.at[n, me],
            device_id=(video, target),
            device_id_type=MESH,
        )

    def second_arrival(n, source):
        lanes = pl.ds(chunks[n][0], chunks[n][1])
        return pltpu.make_async_remote_copy(
            src_ref=out2_ref.at[rows_of(source), lanes],
            dst_ref=o_ref.at[rows_of(source), lanes],
            send_sem=send2.at[n, source],
            recv_sem=recv2.at[n, source],
            device_id=(video, source),
            device_id_type=MESH,
        )

    done = 0
    for n, (first, width) in enumerate(chunks):
        until = -(-(first + width) // HEAD)

        def mix(group, carry, heads=tuple(range(done, until))):
            mix_group(group, heads, xb_ref, y_ref, gram_ref, lead_ref, lead_t_ref, step_t_ref)
            return carry

        lax.fori_loop(0, groups, mix, 0)
        done = until

        def gather(target, first=first, width=width):
            for lane in range(first, first + width, 128):
                out2_ref[rows_of(target), pl.ds(lane, 128)] = y_ref[
                    lane // 128, pl.ds(target, per, stride=frames), :
                ].astype(BF16)

        for turn in range(2):
            side = lax.rem(me // half + 1 + turn, 2)

            def give(k, carry, side=side, n=n, gather=gather):
                target = side * half + lax.rem(me + k, half)
                gather(target)
                second_copy(n, target).start()
                return carry

            lax.fori_loop(turn, half, give, 0)
        gather(me)

    own = pltpu.make_async_copy(out2_ref.at[rows_of(me)], o_ref.at[rows_of(me)], own_sem)
    own.start()

    def sent1(k, carry):
        first_copy(lax.rem(me + k, frames)).wait_send()
        return carry

    lax.fori_loop(1, frames, sent1, 0)
    for n in range(len(chunks)):

        def finish(k, carry, n=n):
            second_copy(n, lax.rem(me + k, frames)).wait_send()
            second_arrival(n, lax.rem(me + k, frames)).wait_recv()
            return carry

        lax.fori_loop(1, frames, finish, 0)
    own.wait()


def shards(queries, key_vectors, values_in, norm_gain, state_weight, step_weight, step_bias, decay_rate):
    tokens, channels = queries.shape
    frames = lax.axis_size("seq")
    rows = 4 * frames
    groups = tokens // rows
    block = tokens // 2
    chunks = ((0, 128), (128, 256), (384, 384), (768, 384))
    vmem = pl.BlockSpec(memory_space=pltpu.VMEM)
    hbm = pl.BlockSpec(memory_space=pl.ANY)
    return pl.pallas_call(
        functools.partial(kernel, frames, chunks),
        out_shape=jax.ShapeDtypeStruct((tokens, channels), BF16),
        in_specs=[hbm, hbm, hbm, vmem, vmem, vmem, vmem, vmem],
        out_specs=hbm,
        scratch_shapes=[
            pltpu.VMEM((tokens, channels), BF16),
            pltpu.VMEM((tokens, channels), BF16),
            pltpu.VMEM((tokens, channels), BF16),
            pltpu.VMEM((block, channels), F32),
            pltpu.VMEM((tokens, channels), BF16),
            pltpu.VMEM((tokens, channels), BF16),
            pltpu.VMEM((channels // 128, tokens, 128), F32),
            pltpu.VMEM((tokens, channels), BF16),
            pltpu.VMEM((channels // 128, tokens, 128), F32),
            pltpu.VMEM((groups, 2, rows, rows), F32),
            pltpu.VMEM((groups, rows, 2 * HEADS), F32),
            pltpu.VMEM((groups, 2 * HEADS, rows), F32),
            pltpu.VMEM((groups, 2 * HEADS, rows), F32),
            pltpu.VMEM((tokens, channels), BF16),
            pltpu.SemaphoreType.DMA((3,)),
            pltpu.SemaphoreType.DMA((frames,)),
            pltpu.SemaphoreType.DMA((frames,)),
            pltpu.SemaphoreType.DMA((len(chunks), frames)),
            pltpu.SemaphoreType.DMA((len(chunks), frames)),
            pltpu.SemaphoreType.DMA,
        ],
        compiler_params=pltpu.CompilerParams(
            collective_id=0, has_side_effects=True, vmem_limit_bytes=48 * 2**20
        ),
    )(
        queries, key_vectors, values_in, norm_gain[None], state_weight, step_weight, step_bias[None], decay_rate[None]
    )


def solution(mesh):
    rows = P(("video", "seq"), None)
    return jax.shard_map(
        shards,
        mesh=mesh,
        in_specs=(rows, rows, rows, P(), P(), P(), P(), P()),
        out_specs=rows,
        check_vma=False,
    )
```

time: 243 us -> 140 us (0.58)
  the two profiles are of different devices: /device:TPU:24 before, /device:TPU:48 now
where the time goes in v1:
time: 140 us
  Pallas kernels  131 us (94%)
  local copies, waits for them, and re-layouts  9 us (6%)
    pallas_call x1, Pallas kernels, shards(): pl.pallas_call(functools.partial(kernel, frames, chunks), out_shape=jax.S...  131 us
    unnamed x14, local copies, waits for them, and re-layouts  8.3 us

profile of v1, /device:TPU:48, one launch (start us, length us, event | category | flops | bytes accessed | tf_op | source)
XLA Modules:
  0.0 139.8 jit_solution(14170722971606277280)
XLA Ops:
  0.0 0.7 broadcast_in_dim.9.gain_ref
  0.7 1.1 copy.9.tw_ref
  1.8 0.0 copy-start
  1.8 1.3 copy-done
  3.1 0.0 copy-start.1
  3.1 1.3 copy-done.1
  4.4 0.0 copy-start.2
  4.4 1.3 copy-done.2
  5.6 0.0 copy-start.3
  5.6 1.1 copy-done.3
  6.7 0.0 copy-start.4
  6.7 0.7 copy-done.4
  7.3 0.0 copy-start.5
  7.3 0.7 copy-done.5
  8.0 130.8 %shard_map.82 = bf16[512,1152]{1,0:T(8,128)(2,1)S(1)} custom-call(bf16[512,1152]{1,0:T(8,128)(2,1)S(1)} %copy-done, bf16[512,1152]{1,0:T(8,128)(2,1)S(1)} %copy-done.1, bf16[512,1152]{1,0:T(8,128)(2,1)S(1)} %copy-done.2, f32[1,1152]{1,0:T(1,128)S(1)} %broadcast_in_dim.9.gain_ref, bf16[1152,256]{1,0:T(8,128)(2,1)S(1)} %copy-done.3, ...), custom_call_target="tpu_custom_call" | custom-call | tf_op jit(solution)/shard_map/pallas_call | solution.py:306
  138.8 1.0 copy.11
Async XLA Ops:
  1.8 1.3 copy-start
  3.1 1.3 copy-start.1
  4.4 1.3 copy-start.2
  5.6 1.1 copy-start.3
  6.7 0.7 copy-start.4
  7.3 0.7 copy-start.5

commit v2 on v1

v2 whole, which is shorter than its diff:
```python
import functools

import jax
import jax.numpy as jnp
from jax import lax
from jax.experimental import pallas as pl
from jax.experimental.pallas import tpu as pltpu
from jax.sharding import PartitionSpec as P

HEADS = 16
HEAD = 72
STATE = 64
EPSILON = 1e-06
LOG2E = 1.4426950408889634
WINDOW = 256
MESH = pl.DeviceIdType.MESH
NT = (((1,), (1,)), ((), ()))
F32 = jnp.float32
BF16 = jnp.bfloat16


def window_of(head, channels):
    start = min(head * HEAD // 128 * 128, channels - WINDOW)
    return start, head * HEAD - start


def head_mask(rows, offset):
    lane = lax.broadcasted_iota(jnp.int32, (rows, WINDOW), 1)
    return (lane >= offset) & (lane < offset + HEAD)


def attend(q_ref, k_ref, v_ref, acc_ref, row):
    rows, channels = acc_ref.shape
    scale = HEAD ** (-0.5) * LOG2E
    for head in range(HEADS):
        start, offset = window_of(head, channels)
        lanes = pl.ds(start, WINDOW)
        mask = head_mask(rows, offset)
        query = jnp.where(mask, q_ref[pl.ds(row, rows), lanes], jnp.zeros((), BF16))
        scores = lax.dot_general(query, k_ref[:, lanes], NT, preferred_element_type=F32)
        row_max = jnp.max(scores, axis=1, keepdims=True)
        exponent = jnp.exp2((scores - row_max) * scale)
        total = jnp.sum(exponent, axis=1, keepdims=True)
        probabilities = (exponent * (1.0 / total)).astype(BF16)
        mixed = jnp.dot(probabilities, v_ref[:, lanes], preferred_element_type=F32)
        acc_ref[:, lanes] = jnp.where(mask, mixed, acc_ref[:, lanes])


def normalize(attended, gain):
    widened = attended.astype(BF16).astype(F32)
    mean_square = jnp.mean(widened * widened, axis=1, keepdims=True)
    return (widened * lax.rsqrt(mean_square + EPSILON) * gain).astype(BF16)


def prepare_group(group, proj_ref, bias_ref, decay_ref, gram_ref, lead_ref, lead_t_ref, step_t_ref):
    rows = gram_ref.shape[2]
    frames = rows // 4
    base = pl.ds(pl.multiple_of(group * rows, rows), rows)
    i = lax.broadcasted_iota(jnp.int32, (rows, rows), 0)
    j = lax.broadcasted_iota(jnp.int32, (rows, rows), 1)
    same = (i // frames) == (j // frames)
    causal, anti = same & (j <= i), same & (j >= i)
    for direction, mask in ((0, causal), (1, anti)):
        state = proj_ref[direction, base, :].astype(BF16)
        gram = lax.dot_general(state[:, STATE:], state[:, :STATE], NT, preferred_element_type=F32)
        gram_ref[group, direction] = jnp.where(mask, gram * STATE ** (-0.5), 0.0)
    step = proj_ref[2, base, : 2 * HEADS] + bias_ref[...]
    step = jnp.maximum(step, 0.0) + jnp.log1p(jnp.exp(-jnp.abs(step)))
    high = step.astype(BF16)
    low = (step - high.astype(F32)).astype(BF16)
    sums = []
    for mask in (causal, anti):
        ones = jnp.where(mask, 1.0, 0.0).astype(BF16)
        sums.append(
            jnp.dot(ones, high, preferred_element_type=F32) + jnp.dot(ones, low, preferred_element_type=F32)
        )
    column = lax.broadcasted_iota(jnp.int32, step.shape, 1)
    lead = jnp.where(column < HEADS, sums[0], sums[1]) * (decay_ref[...] * LOG2E)
    lead_ref[group] = lead
    lead_t_ref[group] = lead.T
    step_t_ref[group] = step.T


def mix_group(group, heads, tiles, x_ref, xb_ref, y_ref, gram_ref, lead_ref, lead_t_ref, step_t_ref):
    rows = gram_ref.shape[2]
    channels = xb_ref.shape[1]
    base = pl.ds(pl.multiple_of(group * rows, rows), rows)
    for tile in tiles:
        xb_ref[base, pl.ds(tile * 128, 128)] = x_ref[tile, base, :].astype(BF16)
    i = lax.broadcasted_iota(jnp.int32, (rows, rows), 0)
    j = lax.broadcasted_iota(jnp.int32, (rows, rows), 1)
    causal = j <= i
    for head in heads:
        back = HEADS + head
        gap = jnp.where(
            causal,
            lead_t_ref[group, head : head + 1, :] - lead_ref[group, :, head : head + 1],
            lead_t_ref[group, back : back + 1, :] - lead_ref[group, :, back : back + 1],
        )
        weight = jnp.exp2(jnp.minimum(gap, 0.0)) * (
            gram_ref[group, 0] * step_t_ref[group, head : head + 1, :]
            + gram_ref[group, 1] * step_t_ref[group, back : back + 1, :]
        )
        start, offset = window_of(head, channels)
        normed = xb_ref[base, pl.ds(start, WINDOW)]
        mixed = jnp.dot(weight.astype(BF16), normed, preferred_element_type=F32) + normed.astype(F32)
        mask = head_mask(rows, offset)
        for side in range(WINDOW // 128):
            own = slice(side * 128, side * 128 + 128)
            if offset < own.stop and offset + HEAD > own.start:
                place = (start // 128 + side, base, slice(None))
                y_ref[place] = jnp.where(mask[:, own], mixed[:, own], y_ref[place])


def kernel(
    frames, chunks,
    q_hbm, k_hbm, v_hbm, sw_hbm, tw_hbm, gain_ref, bias_ref, decay_ref, o_ref,
    q_ref, k_ref, v_ref, sw_ref, tw_ref, acc_ref, out1_ref, in1_ref, x_ref, xb_ref, y_ref, proj_ref,
    gram_ref, lead_ref, lead_t_ref, step_t_ref, out2_ref,
    q_sem, in_sem, send1, recv1, send2, recv2, own_sem,
):
    video, me = lax.axis_index("video"), lax.axis_index("seq")
    tokens, channels = out1_ref.shape
    per = tokens // frames
    ring = frames // 2
    my_ring, my_side = me // 2, lax.rem(me, 2)
    block = acc_ref.shape[0]
    tiles = channels // 128

    half = ring // 2
    my_parity = lax.rem(my_ring, 2)

    def shift(place):
        return half + jnp.where(lax.rem(place, 2) == 0, place // 2, -((place + 1) // 2))

    def device_at(distance, side):
        return 2 * lax.rem(my_ring + distance, ring) + side

    def peer(n):
        return device_at(shift(n // 2), lax.rem(n, 2))

    def slot_at(distance):
        back = lax.rem(ring - distance, ring)
        place = jnp.where(back >= half, 2 * (back - half), 2 * (half - back) - 1)
        return 2 * place + my_side

    def first_shift(place):
        step = lax.rem(place, half)
        up = lax.rem(step + place // half + my_parity, 2) == 0
        return jnp.where(up, half + step, half - 1 - step)

    def rows_of(index):
        return pl.ds(pl.multiple_of(index * per, per), per)

    def load_queries(place):
        rows = 2 * per
        source = lax.rem(my_ring + first_shift(place), ring)
        return pltpu.make_async_copy(
            q_hbm.at[pl.ds(pl.multiple_of(source * rows, rows), rows)],
            q_ref.at[pl.ds(pl.multiple_of(place * rows, rows), rows)],
            q_sem.at[place],
        )

    def each(low, high, body):
        def step(n, carry):
            body(n)
            return carry

        lax.fori_loop(low, high, step, 0)

    loads = [
        pltpu.make_async_copy(source, target, in_sem.at[n])
        for n, (source, target) in enumerate(
            ((k_hbm, k_ref), (v_hbm, v_ref), (sw_hbm, sw_ref), (tw_hbm, tw_ref))
        )
    ]
    loads[0].start()
    each(0, ring, lambda place: load_queries(place).start())
    for load in loads[1:]:
        load.start()
    barrier = pltpu.get_barrier_semaphore()
    each(
        1,
        frames,
        lambda k: pl.semaphore_signal(
            barrier, inc=1, device_id=(video, lax.rem(me + k, frames)), device_id_type=MESH
        ),
    )
    each(0, ring, lambda place: load_queries(place).wait())
    for load in loads:
        load.wait()

    def first_copy(n):
        distance = first_shift(n // 2)
        there = slot_at(distance)
        return pltpu.make_async_remote_copy(
            src_ref=out1_ref.at[rows_of(n)],
            dst_ref=in1_ref.at[rows_of(there)],
            send_sem=send1.at[n],
            recv_sem=recv1.at[there],
            device_id=(video, device_at(distance, lax.rem(n, 2))),
            device_id_type=MESH,
        )

    def first_arrival(n):
        return pltpu.make_async_remote_copy(
            src_ref=out1_ref.at[rows_of(n)],
            dst_ref=in1_ref.at[rows_of(n)],
            send_sem=send1.at[n],
            recv_sem=recv1.at[n],
            device_id=(video, peer(n)),
            device_id_type=MESH,
        )

    own_slot = frames - 2 + my_side
    own_first = 2 * (half * my_parity + half - 1) + my_side

    def remote(n, action, own=own_slot):
        @pl.when(n != own)
        def _():
            action(n)

    def remote_first(n, action):
        remote(n, action, own_first)

    per_block = block // per

    def first_part(turn):
        row = pl.multiple_of(turn * block, block)
        attend(q_ref, k_ref, v_ref, acc_ref, row)
        out1_ref[pl.ds(row, block), :] = normalize(acc_ref[...], gain_ref[...][None])

        @pl.when(turn == 0)
        def _():
            pl.semaphore_wait(barrier, frames - 1)

        each(turn * per_block, (turn + 1) * per_block, lambda n: remote_first(n, lambda n: first_copy(n).start()))

    each(0, tokens // block, first_part)
    in1_ref[rows_of(own_slot), :] = out1_ref[rows_of(own_first), :]

    groups, rows = gram_ref.shape[0], gram_ref.shape[2]

    def arrive(batch):
        for k in range(rows // per):
            n = batch * (rows // per) + k
            remote(n, lambda n: first_arrival(n).wait_recv())
        arrived = in1_ref[pl.ds(pl.multiple_of(batch * rows, rows), rows), :]
        state = jnp.dot(arrived, sw_ref[...], preferred_element_type=F32).astype(BF16).astype(F32)
        step = lax.dot_general(arrived, tw_ref[...], NT, preferred_element_type=F32).astype(BF16).astype(F32)
        for k in range(rows // per):
            n = batch * (rows // per) + k
            place = pl.ds(peer(n), per, stride=frames)
            here = slice(k * per, k * per + per)
            wide = in1_ref[rows_of(n), :].astype(F32)
            for tile in range(tiles):
                x_ref[tile, place, :] = wide[:, tile * 128 : tile * 128 + 128]
            proj_ref[0, place, :] = state[here, :128]
            proj_ref[1, place, :] = state[here, 128:]
            proj_ref[2, place, :] = jnp.concatenate([step[here]] * (128 // step.shape[1]), axis=1)

    each(0, groups, arrive)
    each(
        0,
        groups,
        lambda group: prepare_group(
            group, proj_ref, bias_ref, decay_ref, gram_ref, lead_ref, lead_t_ref, step_t_ref
        ),
    )

    def second_copy(c, n):
        lanes = pl.ds(chunks[c][0], chunks[c][1])
        return pltpu.make_async_remote_copy(
            src_ref=out2_ref.at[rows_of(n), lanes],
            dst_ref=o_ref.at[rows_of(me), lanes],
            send_sem=send2.at[c, n],
            recv_sem=recv2.at[c, slot_at(shift(n // 2))],
            device_id=(video, peer(n)),
            device_id_type=MESH,
        )

    def second_arrival(c, n):
        lanes = pl.ds(chunks[c][0], chunks[c][1])
        return pltpu.make_async_remote_copy(
            src_ref=out2_ref.at[rows_of(n), lanes],
            dst_ref=o_ref.at[rows_of(peer(n)), lanes],
            send_sem=send2.at[c, n],
            recv_sem=recv2.at[c, n],
            device_id=(video, peer(n)),
            device_id_type=MESH,
        )

    done, wide_done = 0, 0
    for c, (first, width) in enumerate(chunks):
        until = -(-(first + width) // HEAD)
        wide_until = (window_of(until - 1, channels)[0] + WINDOW) // 128
        heads, wide = range(done, until), range(wide_done, wide_until)
        done, wide_done = until, wide_until
        each(
            0,
            groups,
            lambda group, heads=heads, wide=wide: mix_group(
                group, heads, wide, x_ref, xb_ref, y_ref, gram_ref, lead_ref, lead_t_ref, step_t_ref
            ),
        )

        def give(n, c=c, first=first, width=width):
            for lane in range(first, first + width, 128):
                out2_ref[rows_of(n), pl.ds(lane, 128)] = y_ref[
                    lane // 128, pl.ds(peer(n), per, stride=frames), :
                ].astype(BF16)
            remote(n, lambda n: second_copy(c, n).start())

        each(0, frames, give)

    own = pltpu.make_async_copy(out2_ref.at[rows_of(own_slot)], o_ref.at[rows_of(me)], own_sem)
    own.start()
    each(0, frames, lambda n: remote_first(n, lambda n: first_copy(n).wait_send()))
    for c in range(len(chunks)):

        def finish(n, c=c):
            second_copy(c, n).wait_send()
            second_arrival(c, n).wait_recv()

        each(0, frames, lambda n, finish=finish: remote(n, finish))
    own.wait()


def shards(queries, key_vectors, values_in, norm_gain, state_weight, step_weight, step_bias, decay_rate):
    tokens, channels = queries.shape
    frames = lax.axis_size("seq")
    rows = 4 * frames
    groups = tokens // rows
    block = tokens // 2
    chunks = ((0, 128), (128, 256), (384, 384), (768, 384))
    vmem = pl.BlockSpec(memory_space=pltpu.VMEM)
    hbm = pl.BlockSpec(memory_space=pltpu.HBM)
    return pl.pallas_call(
        functools.partial(kernel, frames, chunks),
        out_shape=jax.ShapeDtypeStruct((tokens, channels), BF16),
        in_specs=[hbm, hbm, hbm, hbm, hbm, vmem, vmem, vmem],
        out_specs=pl.BlockSpec(memory_space=pl.ANY),
        scratch_shapes=[
            pltpu.VMEM((tokens, channels), BF16),
            pltpu.VMEM((tokens, channels), BF16),
            pltpu.VMEM((tokens, channels), BF16),
            pltpu.VMEM(state_weight.shape, BF16),
            pltpu.VMEM(step_weight.shape[::-1], BF16),
            pltpu.VMEM((block, channels), F32),
            pltpu.VMEM((tokens, channels), BF16),
            pltpu.VMEM((tokens, channels), BF16),
            pltpu.VMEM((channels // 128, tokens, 128), F32),
            pltpu.VMEM((tokens, channels), BF16),
            pltpu.VMEM((channels // 128, tokens, 128), F32),
            pltpu.VMEM((3, tokens, 128), F32),
            pltpu.VMEM((groups, 2, rows, rows), F32),
            pltpu.VMEM((groups, rows, 2 * HEADS), F32),
            pltpu.VMEM((groups, 2 * HEADS, rows), F32),
            pltpu.VMEM((groups, 2 * HEADS, rows), F32),
            pltpu.VMEM((tokens, channels), BF16),
            pltpu.SemaphoreType.DMA((frames // 2,)),
            pltpu.SemaphoreType.DMA((4,)),
            pltpu.SemaphoreType.DMA((frames,)),
            pltpu.SemaphoreType.DMA((frames,)),
            pltpu.SemaphoreType.DMA((len(chunks), frames)),
            pltpu.SemaphoreType.DMA((len(chunks), frames)),
            pltpu.SemaphoreType.DMA,
        ],
        compiler_params=pltpu.CompilerParams(
            collective_id=0, has_side_effects=True, vmem_limit_bytes=62 * 2**20
        ),
    )(
        queries, key_vectors, values_in, state_weight, step_weight.T, norm_gain, step_bias[None], decay_rate[None]
    )


def solution(mesh):
    rows = P(("video", "seq"), None)
    return jax.shard_map(
        shards,
        mesh=mesh,
        in_specs=(rows, rows, rows, P(), P(), P(), P(), P()),
        out_specs=rows,
        check_vma=False,
    )
```

time: 140 us -> 128 us (0.914)
  the two profiles are of different devices: /device:TPU:48 before, /device:TPU:24 now
where the time goes in v2:
time: 128 us
  Pallas kernels  125 us (98%)
  local copies, waits for them, and re-layouts  2.37 us (2%)
    pallas_call x1, Pallas kernels, shards(): pl.pallas_call(functools.partial(kernel, frames, chunks), out_shape=jax.S...  125 us

profile of v2, /device:TPU:24, one launch (start us, length us, event | category | flops | bytes accessed | tf_op | source)
XLA Modules:
  0.0 127.9 jit_solution(11222157942991190629)
XLA Ops:
  0.0 125.5 %shard_map.82 = bf16[512,1152]{1,0:T(8,128)(2,1)} custom-call(bf16[512,1152]{1,0:T(8,128)(2,1)} %q_hbm.1, bf16[512,1152]{1,0:T(8,128)(2,1)} %k_hbm.1, bf16[512,1152]{1,0:T(8,128)(2,1)} %v_hbm.1, bf16[1152,256]{1,0:T(8,128)(2,1)} %sw_hbm.1, bf16[32,1152]{1,0:T(8,128)(2,1)} %bitcast.3, f32[1152]{0:T(1024)} %gain_ref.1, f32[1,32]{1,0:T(1,128)} %bitcast.4, ...), custom_call_target="tpu_custom_call" | custom-call | tf_op jit(solution)/shard_map/pallas_call | solution.py:338
  125.5 2.4 %copy.10 = bf16[512,1152]{1,0:T(8,128)(2,1)} copy(bf16[512,1152]{1,0:T(8,128)(2,1)} %shard_map.82) | data formatting | bytes 2359296

commit v3 on v2

--- a/solution.py
+++ b/solution.py
@@ -174,20 +174,22 @@
             ((k_hbm, k_ref), (v_hbm, v_ref), (sw_hbm, sw_ref), (tw_hbm, tw_ref))
         )
     ]
+    barrier = pltpu.get_barrier_semaphore()
+
+    def greet(k):
+        pl.semaphore_signal(
+            barrier, inc=1, device_id=(video, lax.rem(me + k, frames)), device_id_type=MESH
+        )
+
     loads[0].start()
+    each(half, frames - half, greet)
     each(0, ring, lambda place: load_queries(place).start())
     for load in loads[1:]:
         load.start()
-    barrier = pltpu.get_barrier_semaphore()
-    each(
-        1,
-        frames,
-        lambda k: pl.semaphore_signal(
-            barrier, inc=1, device_id=(video, lax.rem(me + k, frames)), device_id_type=MESH
-        ),
-    )
+    each(1, half, greet)
+    each(frames - half, frames, greet)
     each(0, ring, lambda place: load_queries(place).wait())
-    for load in loads:
+    for load in loads[:2]:
         load.wait()
 
     def first_copy(n):
@@ -259,6 +261,8 @@
             proj_ref[1, place, :] = state[here, 128:]
             proj_ref[2, place, :] = jnp.concatenate([step[here]] * (128 // step.shape[1]), axis=1)
 
+    for load in loads[2:]:
+        load.wait()
     each(0, groups, arrive)
     each(
         0,
@@ -337,9 +341,9 @@
     hbm = pl.BlockSpec(memory_space=pltpu.HBM)
     return pl.pallas_call(
         functools.partial(kernel, frames, chunks),
-        out_shape=jax.ShapeDtypeStruct((tokens, channels), BF16),
+        out_shape=pltpu.VMEM((tokens, channels), BF16),
         in_specs=[hbm, hbm, hbm, hbm, hbm, vmem, vmem, vmem],
-        out_specs=pl.BlockSpec(memory_space=pl.ANY),
+        out_specs=pl.BlockSpec(memory_space=pltpu.VMEM),
         scratch_shapes=[
             pltpu.VMEM((tokens, channels), BF16),
             pltpu.VMEM((tokens, channels), BF16),
@@ -367,7 +371,7 @@
             pltpu.SemaphoreType.DMA,
         ],
         compiler_params=pltpu.CompilerParams(
-            collective_id=0, has_side_effects=True, vmem_limit_bytes=62 * 2**20
+            collective_id=0, has_side_effects=True, vmem_limit_bytes=56 * 2**20
         ),
     )(
         queries, key_vectors, values_in, state_weight, step_weight.T, norm_gain, step_bias[None], decay_rate[None]

time: 128 us -> 127 us (level)
  local copies, waits for them, and re-layouts: 2.37 us -> 1.02 us
    unnamed x1, local copies, waits for them, and re-layouts: 2.37 us -> 1.02 us
where the time goes in v3:
time: 127 us; the launch traced here: 126 us
  Pallas kernels  125 us (98%)
    pallas_call x1, Pallas kernels, shards(): pl.pallas_call(functools.partial(kernel, frames, chunks), out_shape=pltpu...  125 us

profile of v3, /device:TPU:24, one launch (start us, length us, event | category | flops | bytes accessed | tf_op | source)
XLA Modules:
  0.0 126.2 jit_solution(7390849117414194330)
XLA Ops:
  0.0 125.2 %shard_map.82 = bf16[512,1152]{1,0:T(8,128)(2,1)S(1)} custom-call(bf16[512,1152]{1,0:T(8,128)(2,1)} %q_hbm.1, bf16[512,1152]{1,0:T(8,128)(2,1)} %k_hbm.1, bf16[512,1152]{1,0:T(8,128)(2,1)} %v_hbm.1, bf16[1152,256]{1,0:T(8,128)(2,1)} %sw_hbm.1, bf16[32,1152]{1,0:T(8,128)(2,1)} %bitcast.3, f32[1152]{0:T(1024)} %gain_ref.1, f32[1,32]{1,0:T(1,128)} %bitcast.4, ...), custom_call_target="tpu_custom_call" | custom-call | tf_op jit(solution)/shard_map/pallas_call | solution.py:342
  125.2 1.0 copy.10

commit v4 on v3

--- a/solution.py
+++ b/solution.py
@@ -29,10 +29,10 @@
     return (lane >= offset) & (lane < offset + HEAD)
 
 
-def attend(q_ref, k_ref, v_ref, acc_ref, row):
+def attend(heads, q_ref, k_ref, v_ref, acc_ref, row):
     rows, channels = acc_ref.shape
     scale = HEAD ** (-0.5) * LOG2E
-    for head in range(HEADS):
+    for head in heads:
         start, offset = window_of(head, channels)
         lanes = pl.ds(start, WINDOW)
         mask = head_mask(rows, offset)
@@ -55,7 +55,7 @@
 def prepare_group(group, proj_ref, bias_ref, decay_ref, gram_ref, lead_ref, lead_t_ref, step_t_ref):
     rows = gram_ref.shape[2]
     frames = rows // 4
-    base = pl.ds(pl.multiple_of(group * rows, rows), rows)
+    base = pl.ds(group * rows if isinstance(group, int) else pl.multiple_of(group * rows, rows), rows)
     i = lax.broadcasted_iota(jnp.int32, (rows, rows), 0)
     j = lax.broadcasted_iota(jnp.int32, (rows, rows), 1)
     same = (i // frames) == (j // frames)
@@ -84,7 +84,7 @@
 def mix_group(group, heads, tiles, x_ref, xb_ref, y_ref, gram_ref, lead_ref, lead_t_ref, step_t_ref):
     rows = gram_ref.shape[2]
     channels = xb_ref.shape[1]
-    base = pl.ds(pl.multiple_of(group * rows, rows), rows)
+    base = pl.ds(group * rows if isinstance(group, int) else pl.multiple_of(group * rows, rows), rows)
     for tile in tiles:
         xb_ref[base, pl.ds(tile * 128, 128)] = x_ref[tile, base, :].astype(BF16)
     i = lax.broadcasted_iota(jnp.int32, (rows, rows), 0)
@@ -113,7 +113,7 @@
 
 
 def kernel(
-    frames, chunks,
+    frames, firsts, chunks,
     q_hbm, k_hbm, v_hbm, sw_hbm, tw_hbm, gain_ref, bias_ref, decay_ref, o_ref,
     q_ref, k_ref, v_ref, sw_ref, tw_ref, acc_ref, out1_ref, in1_ref, x_ref, xb_ref, y_ref, proj_ref,
     gram_ref, lead_ref, lead_t_ref, step_t_ref, out2_ref,
@@ -128,7 +128,6 @@
     tiles = channels // 128
 
     half = ring // 2
-    my_parity = lax.rem(my_ring, 2)
 
     def shift(place):
         return half + jnp.where(lax.rem(place, 2) == 0, place // 2, -((place + 1) // 2))
@@ -144,21 +143,17 @@
         place = jnp.where(back >= half, 2 * (back - half), 2 * (half - back) - 1)
         return 2 * place + my_side
 
-    def first_shift(place):
-        step = lax.rem(place, half)
-        up = lax.rem(step + place // half + my_parity, 2) == 0
-        return jnp.where(up, half + step, half - 1 - step)
+    def first_target(n):
+        distance = shift(lax.rem(n, ring))
+        place = lax.rem(my_ring + distance, ring)
+        return distance, 2 * place + lax.rem(place + n // ring, 2)
 
     def rows_of(index):
         return pl.ds(pl.multiple_of(index * per, per), per)
 
-    def load_queries(place):
-        rows = 2 * per
-        source = lax.rem(my_ring + first_shift(place), ring)
+    def load_queries(n):
         return pltpu.make_async_copy(
-            q_hbm.at[pl.ds(pl.multiple_of(source * rows, rows), rows)],
-            q_ref.at[pl.ds(pl.multiple_of(place * rows, rows), rows)],
-            q_sem.at[place],
+            q_hbm.at[rows_of(first_target(n)[1])], q_ref.at[rows_of(n)], q_sem.at[n]
         )
 
     def each(low, high, body):
@@ -183,39 +178,42 @@
 
     loads[0].start()
     each(half, frames - half, greet)
-    each(0, ring, lambda place: load_queries(place).start())
-    for load in loads[1:]:
+    each(0, ring, lambda n: load_queries(n).start())
+    loads[1].start()
+    each(ring, frames, lambda n: load_queries(n).start())
+    for load in loads[2:]:
         load.start()
     each(1, half, greet)
     each(frames - half, frames, greet)
-    each(0, ring, lambda place: load_queries(place).wait())
     for load in loads[:2]:
         load.wait()
 
-    def first_copy(n):
-        distance = first_shift(n // 2)
+    def first_copy(c, n):
+        distance, target = first_target(n)
         there = slot_at(distance)
+        lanes = pl.ds(firsts[c][0], firsts[c][1])
         return pltpu.make_async_remote_copy(
-            src_ref=out1_ref.at[rows_of(n)],
-            dst_ref=in1_ref.at[rows_of(there)],
-            send_sem=send1.at[n],
-            recv_sem=recv1.at[there],
-            device_id=(video, device_at(distance, lax.rem(n, 2))),
+            src_ref=out1_ref.at[rows_of(n), lanes],
+            dst_ref=in1_ref.at[rows_of(there), lanes],
+            send_sem=send1.at[c, n],
+            recv_sem=recv1.at[c, there],
+            device_id=(video, target),
             device_id_type=MESH,
         )
 
-    def first_arrival(n):
+    def first_arrival(c, n):
+        lanes = pl.ds(firsts[c][0], firsts[c][1])
         return pltpu.make_async_remote_copy(
-            src_ref=out1_ref.at[rows_of(n)],
-            dst_ref=in1_ref.at[rows_of(n)],
-            send_sem=send1.at[n],
-            recv_sem=recv1.at[n],
+            src_ref=out1_ref.at[rows_of(n), lanes],
+            dst_ref=in1_ref.at[rows_of(n), lanes],
+            send_sem=send1.at[c, n],
+            recv_sem=recv1.at[c, n],
             device_id=(video, peer(n)),
             device_id_type=MESH,
         )
 
     own_slot = frames - 2 + my_side
-    own_first = 2 * (half * my_parity + half - 1) + my_side
+    own_first = lax.rem(my_ring + my_side, 2) * ring + ring - 1
 
     def remote(n, action, own=own_slot):
         @pl.when(n != own)
@@ -229,14 +227,24 @@
 
     def first_part(turn):
         row = pl.multiple_of(turn * block, block)
-        attend(q_ref, k_ref, v_ref, acc_ref, row)
-        out1_ref[pl.ds(row, block), :] = normalize(acc_ref[...], gain_ref[...][None])
-
-        @pl.when(turn == 0)
-        def _():
-            pl.semaphore_wait(barrier, frames - 1)
-
-        each(turn * per_block, (turn + 1) * per_block, lambda n: remote_first(n, lambda n: first_copy(n).start()))
+        each(turn * ring, (turn + 1) * ring, lambda n: load_queries(n).wait())
+        done = 0
+        for c, (first, width) in enumerate(firsts):
+            until = -(-(first + width) // HEAD)
+            attend(range(done, until), q_ref, k_ref, v_ref, acc_ref, row)
+            done = until
+            lanes = pl.ds(first, width)
+            out1_ref[pl.ds(row, block), lanes] = acc_ref[:, lanes].astype(BF16)
+            if c == 0:
+
+                @pl.when(turn == 0)
+                def _():
+                    pl.semaphore_wait(barrier, frames - 1)
+
+            def send(n, c=c):
+                remote_first(n, lambda n: first_copy(c, n).start())
+
+            each(turn * per_block, (turn + 1) * per_block, send)
 
     each(0, tokens // block, first_part)
     in1_ref[rows_of(own_slot), :] = out1_ref[rows_of(own_first), :]
@@ -246,15 +254,16 @@
     def arrive(batch):
         for k in range(rows // per):
             n = batch * (rows // per) + k
-            remote(n, lambda n: first_arrival(n).wait_recv())
-        arrived = in1_ref[pl.ds(pl.multiple_of(batch * rows, rows), rows), :]
+            for c in range(len(firsts)):
+                remote(n, lambda n, c=c: first_arrival(c, n).wait_recv())
+        arrived = normalize(in1_ref[pl.ds(pl.multiple_of(batch * rows, rows), rows), :], gain_ref[...][None])
         state = jnp.dot(arrived, sw_ref[...], preferred_element_type=F32).astype(BF16).astype(F32)
         step = lax.dot_general(arrived, tw_ref[...], NT, preferred_element_type=F32).astype(BF16).astype(F32)
         for k in range(rows // per):
             n = batch * (rows // per) + k
             place = pl.ds(peer(n), per, stride=frames)
             here = slice(k * per, k * per + per)
-            wide = in1_ref[rows_of(n), :].astype(F32)
+            wide = arrived[here].astype(F32)
             for tile in range(tiles):
                 x_ref[tile, place, :] = wide[:, tile * 128 : tile * 128 + 128]
             proj_ref[0, place, :] = state[here, :128]
@@ -264,13 +273,8 @@
     for load in loads[2:]:
         load.wait()
     each(0, groups, arrive)
-    each(
-        0,
-        groups,
-        lambda group: prepare_group(
-            group, proj_ref, bias_ref, decay_ref, gram_ref, lead_ref, lead_t_ref, step_t_ref
-        ),
-    )
+    for group in range(groups):
+        prepare_group(group, proj_ref, bias_ref, decay_ref, gram_ref, lead_ref, lead_t_ref, step_t_ref)
 
     def second_copy(c, n):
         lanes = pl.ds(chunks[c][0], chunks[c][1])
@@ -300,13 +304,17 @@
         wide_until = (window_of(until - 1, channels)[0] + WINDOW) // 128
         heads, wide = range(done, until), range(wide_done, wide_until)
         done, wide_done = until, wide_until
-        each(
-            0,
-            groups,
-            lambda group, heads=heads, wide=wide: mix_group(
+
+        def mix(group, heads=heads, wide=wide):
+            mix_group(
                 group, heads, wide, x_ref, xb_ref, y_ref, gram_ref, lead_ref, lead_t_ref, step_t_ref
-            ),
-        )
+            )
+
+        if c == 0:
+            for group in range(groups):
+                mix(group)
+        else:
+            each(0, groups, mix)
 
         def give(n, c=c, first=first, width=width):
             for lane in range(first, first + width, 128):
@@ -319,7 +327,8 @@
 
     own = pltpu.make_async_copy(out2_ref.at[rows_of(own_slot)], o_ref.at[rows_of(me)], own_sem)
     own.start()
-    each(0, frames, lambda n: remote_first(n, lambda n: first_copy(n).wait_send()))
+    for c in range(len(firsts)):
+        each(0, frames, lambda n, c=c: remote_first(n, lambda n: first_copy(c, n).wait_send()))
     for c in range(len(chunks)):
 
         def finish(n, c=c):
@@ -336,11 +345,12 @@
     rows = 4 * frames
     groups = tokens // rows
     block = tokens // 2
+    firsts = ((0, 640), (640, 512))
     chunks = ((0, 128), (128, 256), (384, 384), (768, 384))
     vmem = pl.BlockSpec(memory_space=pltpu.VMEM)
     hbm = pl.BlockSpec(memory_space=pltpu.HBM)
     return pl.pallas_call(
-        functools.partial(kernel, frames, chunks),
+        functools.partial(kernel, frames, firsts, chunks),
         out_shape=pltpu.VMEM((tokens, channels), BF16),
         in_specs=[hbm, hbm, hbm, hbm, hbm, vmem, vmem, vmem],
         out_specs=pl.BlockSpec(memory_space=pltpu.VMEM),
@@ -362,10 +372,10 @@
             pltpu.VMEM((groups, 2 * HEADS, rows), F32),
             pltpu.VMEM((groups, 2 * HEADS, rows), F32),
             pltpu.VMEM((tokens, channels), BF16),
-            pltpu.SemaphoreType.DMA((frames // 2,)),
+            pltpu.SemaphoreType.DMA((frames,)),
             pltpu.SemaphoreType.DMA((4,)),
-            pltpu.SemaphoreType.DMA((frames,)),
-            pltpu.SemaphoreType.DMA((frames,)),
+            pltpu.SemaphoreType.DMA((len(firsts), frames)),
+            pltpu.SemaphoreType.DMA((len(firsts), frames)),
             pltpu.SemaphoreType.DMA((len(chunks), frames)),
             pltpu.SemaphoreType.DMA((len(chunks), frames)),
             pltpu.SemaphoreType.DMA,

time: 127 us -> 125 us (0.984)
    pallas_call x1, Pallas kernels: 125 us -> 124 us  [shards(): pl.pallas_call(functools.partial(kernel, frames, firsts, chunks), out_sha...]
where the time goes in v4:
time: 125 us
  Pallas kernels  124 us (99%)
    pallas_call x1, Pallas kernels, shards(): pl.pallas_call(functools.partial(kernel, frames, firsts, chunks), out_sha...  124 us

profile of v4, /device:TPU:24, one launch (start us, length us, event | category | flops | bytes accessed | tf_op | source)
XLA Modules:
  0.0 124.7 jit_solution(10021696332172725696)
XLA Ops:
  0.0 123.7 %shard_map.82 = bf16[512,1152]{1,0:T(8,128)(2,1)S(1)} custom-call(bf16[512,1152]{1,0:T(8,128)(2,1)} %q_hbm.1, bf16[512,1152]{1,0:T(8,128)(2,1)} %k_hbm.1, bf16[512,1152]{1,0:T(8,128)(2,1)} %v_hbm.1, bf16[1152,256]{1,0:T(8,128)(2,1)} %sw_hbm.1, bf16[32,1152]{1,0:T(8,128)(2,1)} %bitcast.3, f32[1152]{0:T(1024)} %gain_ref.1, f32[1,32]{1,0:T(1,128)} %bitcast.4, ...), custom_call_target="tpu_custom_call" | custom-call | tf_op jit(solution)/shard_map/pallas_call | solution.py:352
  123.7 1.0 copy.10
